TPU v7x, 32 devices: a whole 2x2x4 slice. The times are simulated.
32 devices in a mesh: groups: 2 (over x), row: 4 (over y, core), dp: 4 (over z).
Axes of the slice: x: 2, y: 2, z: 4, core: 2. Of those that a mesh axis runs over, the one named last changes fastest.
Arguments:
- snapshots: bfloat16 [1024, 4096], P(('groups', 'dp'), 'row'), parts along dimension 0, may hold values from -6 to 6
- enc_weight: bfloat16 [32, 128, 256], P(('row', 'dp')), may hold values from -0.09375 to 0.09375
- hidden_weight: bfloat16 [8192, 256], P('dp'), may hold values from -0.375 to 0.375
- hidden_bias: bfloat16 [8192], P('dp'), may hold values from -3 to 3
- block_weight: bfloat16 [32, 8, 128, 128], P(('row', 'dp')), may hold values from -0.25 to 0.25
- block_ids: int32 [32, 8], P('row'), may hold values from 0 to 63, all different within a row
- block_counts: int32 [32], P('row'), may hold values from 1 to 8, as said below
Outputs:
- enc_grad: float32 [64, 128, 256], P(('groups', 'row', 'dp')), parts along dimension 0
- hidden_weight_grad: float32 [16384, 256], P(('groups', 'dp')), parts along dimension 0
- hidden_bias_grad: float32 [16384], P(('groups', 'dp')), parts along dimension 0
- block_grad: float32 [64, 8, 128, 128], P(('groups', 'row', 'dp')), parts along dimension 0
There are 2 independent parts, one for each index of `groups`. A program takes and returns all parts, laid end to end along the dimension named above; an argument that names none is the same for every part. Nothing has to cross between parts.
Inputs may be any that keep to these rules, and one draw needn't show every extreme that they name: `block_ids`: the 8 block numbers of one tile are distinct. `block_counts`: the live slots of a tile are its first ones; some tile has all 8 live.
All inputs are finite; a program needn't handle non-finite values.
Results may differ from a plain program's by a relative error of at most 0.0043.
Values may be sent and summed in bfloat16 or wider, within the bound.
A program may use at most 128 MiB of HBM per device.

v0:
```python
import math
import jax
import jax.numpy as jnp
from jax import lax
from jax.sharding import PartitionSpec as P


def silu_slope(pre):
    sigma = jax.nn.sigmoid(pre)
    return sigma * (1.0 + pre * (1.0 - sigma))


def on_device(
    snapshots, enc_weight, hidden_weight, hidden_bias, block_weight, block_ids, block_counts
):
    batch, width_rows = snapshots.shape
    enc_all, block_all = (
        lax.all_gather(enc_weight, "dp", axis=0, tiled=True),
        lax.all_gather(block_weight, "dp", axis=0, tiled=True),
    )
    tiles = block_all.shape[0]
    blocks = block_all.shape[1]
    blk_size = block_all.shape[2]
    latent_dim = enc_all.shape[2]
    partial_latent = jnp.dot(
        snapshots, enc_all.reshape(width_rows, latent_dim), preferred_element_type=jnp.float32
    )
    latent = lax.psum(partial_latent, "row")
    latent_b = latent.astype(jnp.bfloat16)
    weight_all, bias_all = (
        lax.all_gather(hidden_weight, "dp", axis=0, tiled=True),
        lax.all_gather(hidden_bias, "dp", axis=0, tiled=True),
    )
    hidden_units = weight_all.shape[0]
    nblocks = hidden_units // blk_size
    pre = lax.dot_general(
        latent_b, weight_all, (((1,), (1,)), ((), ())), preferred_element_type=jnp.float32
    ) + bias_all.astype(jnp.float32)
    hidden = jax.nn.silu(pre).astype(jnp.bfloat16)
    live_slots = jnp.arange(blocks)[None, :] < block_counts[:, None]
    live_float = live_slots.astype(jnp.float32)
    tile_hidden = (
        jnp.take(hidden.reshape(batch, nblocks, blk_size), block_ids, axis=1)
        * live_slots.astype(jnp.bfloat16)[None, :, :, None]
    )
    output = jnp.einsum(
        "btkc,tkcd->btd", tile_hidden, block_all, preferred_element_type=jnp.float32
    )
    scale = 1.0 / math.sqrt(batch * lax.axis_size("dp"))
    snap_tiles = snapshots.reshape(batch, tiles, blk_size).astype(jnp.float32)
    misfit = ((output - snap_tiles) * scale).astype(jnp.bfloat16)
    back = (
        jnp.einsum("btd,tkcd->btkc", misfit, block_all, preferred_element_type=jnp.float32)
        * live_float[None, :, :, None]
    )
    onehot = (block_ids[:, :, None] == jnp.arange(nblocks)[None, None, :]).astype(jnp.float32)
    partial_adjoint = jnp.einsum(
        "btkc,tkn->bnc", back, onehot, precision=lax.Precision.HIGHEST
    ).reshape(batch, hidden_units)
    adjoint = lax.psum(partial_adjoint, "row")
    pre_grad = (adjoint * silu_slope(pre)).astype(jnp.bfloat16)
    bias_part = jnp.sum(pre_grad, axis=0, dtype=jnp.float32)
    weight_part = lax.dot_general(
        pre_grad, latent_b, (((0,), (0,)), ((), ())), preferred_element_type=jnp.float32
    )
    latent_grad = jnp.dot(pre_grad, weight_all, preferred_element_type=jnp.float32).astype(
        jnp.bfloat16
    )
    enc_part = lax.dot_general(
        snapshots, latent_grad, (((0,), (0,)), ((), ())), preferred_element_type=jnp.float32
    ).reshape(tiles, blk_size, latent_dim)
    block_part = jnp.einsum(
        "btkc,btd->tkcd", tile_hidden, misfit, preferred_element_type=jnp.float32
    )
    enc_grad, block_grad, weight_grad, bias_grad = (
        lax.psum_scatter(enc_part, "dp", scatter_dimension=0, tiled=True),
        lax.psum_scatter(block_part, "dp", scatter_dimension=0, tiled=True),
        lax.psum_scatter(weight_part, "dp", scatter_dimension=0, tiled=True),
        lax.psum_scatter(bias_part, "dp", scatter_dimension=0, tiled=True),
    )
    return (enc_grad, weight_grad, bias_grad, block_grad)


def solution(mesh):
    in_specs = (
        P(("groups", "dp"), "row"),
        P(("row", "dp"), None, None),
        P("dp", None),
        P("dp"),
        P(("row", "dp"), None, None, None),
        P("row", None),
        P("row"),
    )
    out_specs = (
        P(("groups", "row", "dp"), None, None),
        P(("groups", "dp"), None),
        P(("groups", "dp")),
        P(("groups", "row", "dp"), None, None, None),
    )
    return jax.shard_map(
        on_device, mesh=mesh, in_specs=in_specs, out_specs=out_specs, check_vma=False
    )
```

profile of v0, /device:TPU:0, one launch (start us, length us, event | category | flops | bytes accessed | tf_op | source)
XLA Modules:
  0.0 510.9 jit_solution(17323204640776790621)
XLA Ops:
  7.2 0.7 all-gather.3.cloned.1.call-update
  8.0 0.7 all-gather.5.cloned.1.call-update
  8.7 1.1 copy.28
  9.8 21.0 %all_gather.12 = bf16[8,128,256]{2,1,0:T(8,128)(2,1)S(1)} all-gather(bf16[2,128,256]{2,1,0:T(8,128)(2,1)} %param.8), channel_id=1, replica_groups=mesh['groups'=2,'row'=4,'dp'=4] {'dp'}, dimensions={0}, use_global_device_ids=true | all-gather | bytes 655360 | tf_op jit(solution)/shard_map/all_gather | solution.py:18
  30.8 1.2 fusion.36
  32.0 14.2 %all_gather.14 = bf16[8192]{0:T(1024)(128)(2,1)S(1)} all-gather(bf16[2048]{0:T(1024)(128)(2,1)} %param.10), channel_id=1, replica_groups=mesh['groups'=2,'row'=4,'dp'=4] {'dp'}, dimensions={0}, use_global_device_ids=true | all-gather | bytes 20480 | tf_op jit(solution)/shard_map/all_gather | solution.py:32
  46.2 0.8 copy.24
  46.9 0.7 compare_select_fusion
  47.9 12.4 %all-reduce.5 = bf16[128,256]{1,0:T(8,128)(2,1)S(1)} all-reduce(f32[128,256]{1,0:T(8,128)S(1)} %fusion.36), channel_id=1, replica_groups=mesh['groups'=2,'row'=4,'dp'=4] {'row'}, use_global_device_ids=true, to_apply=%region_0.0 | all-reduce | flops 32768 | bytes 196608 | tf_op jit(solution)/shard_map/psum | solution.py:28
  60.3 34.9 %all-gather.3.cloned.1.call-done = bf16[8192,256]{1,0:T(8,128)(2,1)} async-done(((bf16[2048,256]{1,0:T(8,128)(2,1)}), bf16[8192,256]{1,0:T(8,128)(2,1)}) %all-gather.3.cloned.1.call-update) | async-done | bytes 4194320 | tf_op jit(solution)/shard_map/all_gather | solution.py:31
  95.3 3.7 convolution_add_fusion
  98.9 2.0 copy-done
  100.9 1.1 copy_bitcast_fusion.1
  102.0 2.1 gather_fusion
  104.1 3.3 copy.26
  107.4 34.4 %all-gather.5.cloned.1.call-done = bf16[8,8,128,128]{3,2,1,0:T(8,128)(2,1)} async-done(((bf16[2,8,128,128]{3,2,1,0:T(8,128)(2,1)}), bf16[8,8,128,128]{3,2,1,0:T(8,128)(2,1)}) %all-gather.5.cloned.1.call-update) | async-done | bytes 2097168 | tf_op jit(solution)/shard_map/all_gather | solution.py:19
  141.8 2.7 fusion.19
  144.6 0.7 copy-done.4
  145.3 0.7 multiply_bitcast_fusion
  146.0 4.8 fusion
  150.9 5.2 %copy.43 = f32[16,8,64,128]{3,1,2,0:T(8,128)} copy(f32[16,8,64,128]{3,2,1,0:T(8,128)S(1)} %bitcast.72) | data formatting | bytes 8388608
  156.2 84.3 %all-reduce.4.cloned.1.call-done = f32[128,8192]{1,0:T(8,128)} async-done(((f32[128,8192]{1,0:T(8,128)}), f32[128,8192]{1,0:T(8,128)}) %all-reduce.4.cloned.1.call-update) | async-done | bytes 4194320 | tf_op jit(solution)/shard_map/psum | solution.py:60
  240.4 4.3 convert_reduce_fusion
  244.8 3.5 convolution_bitcast_fusion
  248.2 1.4 copy.36
  249.7 4.3 fusion.2
  254.1 4.5 fusion.37
  258.6 0.6 copy-done.7
  260.5 19.6 %all-reduce = f32[8192]{0:T(1024)S(1)} all-reduce(f32[8192]{0:T(1024)S(1)} %get-tuple-element.4), channel_id=4, replica_groups=mesh['groups'=2,'row'=4,'dp'=4] {'dp'}, use_global_device_ids=true, to_apply=%region_5.6.clone | all-reduce | flops 8192 | bytes 65536
  280.1 0.6 dynamic-slice.1
  280.7 75.4 %reduce-scatter.8.cloned.1.call-done = f32[2,8,128,128]{3,2,1,0:T(8,128)} async-done(((f32[8,8,128,128]{3,2,1,0:T(8,128)}), f32[2,8,128,128]{3,2,1,0:T(8,128)}) %reduce-scatter.8.cloned.1.call-update) | async-done | bytes 1048592 | tf_op jit(solution)/shard_map/reduce_scatter | solution.py:77
  356.2 147.9 %reduce-scatter.6.cloned.1.call-done = f32[2048,256]{1,0:T(8,128)} async-done(((f32[8192,256]{1,0:T(8,128)}), f32[2048,256]{1,0:T(8,128)}) %reduce-scatter.6.cloned.1.call-update) | async-done | bytes 2097168 | tf_op jit(solution)/shard_map/reduce_scatter | solution.py:78
  (30 shorter events, 1.2 us)
Async XLA Ops:
  7.2 53.1 %copy-start.5 = (s32[8,8]{1,0:T(8,128)S(1)}, s32[8,8]{1,0:T(8,128)}, u32[]{:S(2)}) copy-start(s32[8,8]{1,0:T(8,128)} %param.12) | copy-start | bytes 772
  7.2 53.1 %copy-start.6 = (s32[8]{0:T(128)S(1)}, s32[8]{0:T(128)}, u32[]{:S(2)}) copy-start(s32[8]{0:T(128)} %param.13) | copy-start | bytes 100
  7.2 88.1 %all-gather.3.cloned.1.call-start = ((), (), s32[]{:S(2)}) async-start(), calls=%async_computation.3 | async-start | bytes 5242880 | tf_op jit(solution)/shard_map/all_gather | solution.py:31
  7.9 133.9 %all-gather.5.cloned.1.call-start = ((), (), s32[]{:S(2)}) async-start(), calls=%async_computation.4 | async-start | bytes 2621440 | tf_op jit(solution)/shard_map/all_gather | solution.py:19
  8.7 231.8 %all-reduce.4.cloned.1.call-start = ((), (), s32[]{:S(2)}) async-start(), calls=%async_computation.5 | async-start | bytes 8388608 | tf_op jit(solution)/shard_map/psum | solution.py:60
  98.9 2.0 copy-start
  107.4 38.6 %copy-start.1 = (bf16[8,8,128,128]{2,3,1,0:T(8,128)(2,1)}, bf16[8,8,128,128]{2,3,1,0:T(8,128)(2,1)S(1)}, u32[]{:S(2)}) copy-start(bf16[8,8,128,128]{2,3,1,0:T(8,128)(2,1)S(1)} %copy.26) | copy-start | bytes 6291460
  141.8 3.5 copy-start.3
  144.6 0.7 copy-start.4
  156.1 88.7 %copy-start.2 = (bf16[128,1024]{1,0:T(8,128)(2,1)S(1)}, bf16[128,1024]{1,0:T(8,128)(2,1)}, u32[]{:S(2)}) copy-start(bf16[128,1024]{1,0:T(8,128)(2,1)} %param.7) | copy-start | bytes 786436
  156.1 124.6 %reduce-scatter.4.cloned.1.call-start = ((), (), s32[]{:S(2)}) async-start(), calls=%async_computation.6 | async-start | bytes 1310720 | tf_op jit(solution)/shard_map/reduce_scatter | solution.py:76
  249.6 106.5 %reduce-scatter.8.cloned.1.call-start = ((), (), s32[]{:S(2)}) async-start(), calls=%async_computation.8 | async-start | bytes 5242880 | tf_op jit(solution)/shard_map/reduce_scatter | solution.py:77
  254.0 250.0 %reduce-scatter.6.cloned.1.call-start = ((), (), s32[]{:S(2)}) async-start(), calls=%async_computation.7 | async-start | bytes 10485760 | tf_op jit(solution)/shard_map/reduce_scatter | solution.py:78
  258.6 0.7 copy-start.7
Sparse Core Ops, SparseCore 0:
  9.6 85.6 all-gather.2
  96.8 44.9 all-gather.4
  156.2 84.1 all-reduce.3
  249.8 28.1 reduce-scatter.3
  280.7 75.4 reduce-scatter.7
  359.1 144.9 reduce-scatter.5
where the time goes:
time: 511 us
  waiting for transfers between devices  378 us (74%)
  blocking collectives  67.1 us (13%)
  matrix products  25.4 us (5%)
  local copies, waits for them, and re-layouts  18.6 us (4%)
  between operations  14.9 us (3%)
  other arithmetic  6.17 us (1%)
    reduce_scatter x1, waiting for transfers between devices, on_device(): lax.psum_scatter(weight_part, 'dp', scatter_dimension=0, tiled=True)  148 us
    psum x1, waiting for transfers between devices, on_device(): adjoint = lax.psum(partial_adjoint, 'row')  84.3 us
    reduce_scatter x1, waiting for transfers between devices, on_device(): lax.psum_scatter(block_part, 'dp', scatter_dimension=0, tiled=True)  75.4 us
    all_gather x1, waiting for transfers between devices, on_device(): lax.all_gather(hidden_weight, 'dp', axis=0, tiled=True)  34.9 us
    all_gather x1, waiting for transfers between devices, on_device(): lax.all_gather(block_weight, 'dp', axis=0, tiled=True)  34.4 us
    all_gather x1, blocking collectives, on_device(): lax.all_gather(enc_weight, 'dp', axis=0, tiled=True)  21 us
    unnamed x1, blocking collectives  19.6 us
    all_gather x1, blocking collectives, on_device(): lax.all_gather(hidden_bias, 'dp', axis=0, tiled=True)  14.2 us
  transfers between devices with their start and end apart: 6, of which 5 were waited for; matrix products, arithmetic and copies ran while one was open for 5% of the time, Pallas kernels for 0%

commit v1 on v0

--- a/solution.py
+++ b/solution.py
@@ -3,6 +3,24 @@
 import jax.numpy as jnp
 from jax import lax
 from jax.sharding import PartitionSpec as P
+
+
+def ring_gather(shard, axis, dim):
+    ways, here, hop = (lax.axis_size(axis), lax.axis_index(axis), shard.shape[dim])
+    shape = [n * ways if d == dim else n for d, n in enumerate(shard.shape)]
+    full = lax.dynamic_update_slice_in_dim(
+        jnp.zeros(shape, shard.dtype), shard, here * hop, axis=dim
+    )
+    going_up = going_down = shard
+    for far in range(1, ways // 2 + 1):
+        going_up = lax.ppermute(going_up, axis, [(d, (d + 1) % ways) for d in range(ways)])
+        full = lax.dynamic_update_slice_in_dim(full, going_up, (here - far) % ways * hop, axis=dim)
+        if 2 * far < ways:
+            going_down = lax.ppermute(going_down, axis, [(d, (d - 1) % ways) for d in range(ways)])
+            full = lax.dynamic_update_slice_in_dim(
+                full, going_down, (here + far) % ways * hop, axis=dim
+            )
+    return full
 
 
 def silu_slope(pre):
@@ -15,7 +33,7 @@
 ):
     batch, width_rows = snapshots.shape
     enc_all, block_all = (
-        lax.all_gather(enc_weight, "dp", axis=0, tiled=True),
+        ring_gather(enc_weight, "dp", 0),
         lax.all_gather(block_weight, "dp", axis=0, tiled=True),
     )
     tiles = block_all.shape[0]

time: 511 us -> 511 us (level)
  blocking collectives: 67.1 us -> 45.7 us
  waiting for transfers between devices: 378 us -> 394 us
  starting transfers between devices: 0.24 us -> 5.47 us
    all_gather x1 -> x0, blocking collectives: 21 us -> none  [on_device(): lax.all_gather(enc_weight, 'dp', axis=0, tiled=True)]
    ppermute x0 -> x3, waiting for transfers between devices: none -> 9.48 us  [the longest x2 9.48 us: ring_gather(): lax.ppermute(going_up, axis, [(d, (d + 1) % ways) for d in range(ways)])]
    all_gather x1, waiting for transfers between devices: 34.9 us -> 41.3 us  [on_device(): lax.all_gather(hidden_weight, 'dp', axis=0, tiled=True)]
    ppermute x0 -> x3, starting transfers between devices: none -> 5.23 us  [the longest x2 3.13 us: ring_gather(): lax.ppermute(going_up, axis, [(d, (d + 1) % ways) for d in range(ways)])]
    unnamed x21 -> x17, local copies, waits for them, and re-layouts: 11.6 us -> 10.9 us
  transfers between devices with their start and end apart: 6 -> 9, of which waited for: 5 -> 6; matrix products, arithmetic and copies ran while one was open for 5% -> 5% of each run, Pallas kernels for 0% -> 0%
where the time goes in v1:
time: 511 us; the launch traced here: 510 us
  waiting for transfers between devices  394 us (77%)
  blocking collectives  45.7 us (9%)
  matrix products  24.6 us (5%)
  local copies, waits for them, and re-layouts  18.8 us (4%)
  between operations  15 us (3%)
  other arithmetic  6.88 us (1%)
  starting transfers between devices  5.47 us (1%)
    reduce_scatter x1, waiting for transfers between devices, on_device(): lax.psum_scatter(weight_part, 'dp', scatter_dimension=0, tiled=True)  148 us
    psum x1, waiting for transfers between devices, on_device(): adjoint = lax.psum(partial_adjoint, 'row')  84.3 us
    reduce_scatter x1, waiting for transfers between devices, on_device(): lax.psum_scatter(block_part, 'dp', scatter_dimension=0, tiled=True)  75.5 us
    all_gather x1, waiting for transfers between devices, on_device(): lax.all_gather(hidden_weight, 'dp', axis=0, tiled=True)  41.3 us
    all_gather x1, waiting for transfers between devices, on_device(): lax.all_gather(block_weight, 'dp', axis=0, tiled=True)  34 us
    unnamed x1, blocking collectives  19.6 us
    all_gather x1, blocking collectives, on_device(): lax.all_gather(hidden_bias, 'dp', axis=0, tiled=True)  13.7 us
    psum x1, blocking collectives, on_device(): latent = lax.psum(partial_latent, 'row')  12.4 us
  transfers between devices with their start and end apart: 9, of which 6 were waited for; matrix products, arithmetic and copies ran while one was open for 5% of the time, Pallas kernels for 0%

profile of v1, /device:TPU:0, one launch (start us, length us, event | category | flops | bytes accessed | tf_op | source)
XLA Modules:
  0.0 510.4 jit_solution(14387366140895684670)
XLA Ops:
  7.2 0.7 all-gather.3.cloned.1.call-update
  8.0 0.7 all-gather.5.cloned.1.call-update
  8.7 3.1 collective-permute-start
  11.8 2.1 collective-permute-start.1
  13.9 0.7 compare_select_fusion
  14.6 0.8 fusion.32
  15.4 0.9 constant_dynamic-update-slice_fusion.3
  16.4 0.8 copy.24
  17.2 13.7 %all_gather.10 = bf16[8192]{0:T(1024)(128)(2,1)S(1)} all-gather(bf16[2048]{0:T(1024)(128)(2,1)} %param.10), channel_id=1, replica_groups=mesh['groups'=2,'row'=4,'dp'=4] {'dp'}, dimensions={0}, use_global_device_ids=true | all-gather | bytes 20480 | tf_op jit(solution)/shard_map/all_gather | solution.py:50
  30.9 1.1 copy.28
  32.4 9.5 %collective-permute-done.2 = bf16[2,128,256]{2,1,0:T(8,128)(2,1)S(1)} collective-permute-done((bf16[2,128,256]{2,1,0:T(8,128)(2,1)S(1)}, bf16[2,128,256]{2,1,0:T(8,128)(2,1)S(1)}, u32[]{:S(2)}, u32[]{:S(2)}) %collective-permute-start.2) | collective-permute-done | bytes 131104 | tf_op jit(solution)/shard_map/ppermute | solution.py:16
  42.2 12.4 %all-reduce.5 = bf16[128,256]{0,1:T(8,128)(2,1)S(1)} all-reduce(f32[128,256]{0,1:T(8,128)S(1)} %convolution_bitcast_fusion.1), channel_id=1, replica_groups=mesh['groups'=2,'row'=4,'dp'=4] {'row'}, use_global_device_ids=true, to_apply=%region_0.1 | all-reduce | flops 32768 | bytes 196608 | tf_op jit(solution)/shard_map/psum | solution.py:46
  54.6 41.3 %all-gather.3.cloned.1.call-done = bf16[8192,256]{1,0:T(8,128)(2,1)} async-done(((bf16[2048,256]{1,0:T(8,128)(2,1)}), bf16[8192,256]{1,0:T(8,128)(2,1)}) %all-gather.3.cloned.1.call-update) | async-done | bytes 4194320 | tf_op jit(solution)/shard_map/all_gather | solution.py:49
  95.9 3.7 convolution_add_fusion
  99.6 2.0 copy-done
  101.6 1.1 copy_bitcast_fusion.1
  102.7 2.1 gather_fusion
  104.8 3.2 copy.26
  108.0 34.0 %all-gather.5.cloned.1.call-done = bf16[8,8,128,128]{3,2,1,0:T(8,128)(2,1)} async-done(((bf16[2,8,128,128]{3,2,1,0:T(8,128)(2,1)}), bf16[8,8,128,128]{3,2,1,0:T(8,128)(2,1)}) %all-gather.5.cloned.1.call-update) | async-done | bytes 2097168 | tf_op jit(solution)/shard_map/all_gather | solution.py:37
  142.0 2.7 fusion.19
  144.8 0.7 multiply_bitcast_fusion
  145.5 4.8 fusion
  150.3 5.2 %copy.43 = f32[16,8,64,128]{3,1,2,0:T(8,128)} copy(f32[16,8,64,128]{3,2,1,0:T(8,128)S(1)} %bitcast.74) | data formatting | bytes 8388608
  155.6 84.3 %all-reduce.4.cloned.1.call-done = f32[128,8192]{1,0:T(8,128)} async-done(((f32[128,8192]{1,0:T(8,128)}), f32[128,8192]{1,0:T(8,128)}) %all-reduce.4.cloned.1.call-update) | async-done | bytes 4194320 | tf_op jit(solution)/shard_map/psum | solution.py:78
  239.9 4.3 convert_reduce_fusion
  244.2 3.5 convolution_bitcast_fusion
  247.7 1.4 copy.36
  249.2 4.3 fusion.2
  253.5 4.5 fusion.36
  260.0 19.6 %all-reduce = f32[8192]{0:T(1024)S(1)} all-reduce(f32[8192]{0:T(1024)S(1)} %get-tuple-element.4), channel_id=4, replica_groups=mesh['groups'=2,'row'=4,'dp'=4] {'dp'}, use_global_device_ids=true, to_apply=%region_5.6.clone | all-reduce | flops 8192 | bytes 65536
  280.2 75.5 %reduce-scatter.8.cloned.1.call-done = f32[2,8,128,128]{3,2,1,0:T(8,128)} async-done(((f32[8,8,128,128]{3,2,1,0:T(8,128)}), f32[2,8,128,128]{3,2,1,0:T(8,128)}) %reduce-scatter.8.cloned.1.call-update) | async-done | bytes 1048592 | tf_op jit(solution)/shard_map/reduce_scatter | solution.py:95
  355.6 147.9 %reduce-scatter.6.cloned.1.call-done = f32[2048,256]{1,0:T(8,128)} async-done(((f32[8192,256]{1,0:T(8,128)}), f32[2048,256]{1,0:T(8,128)}) %reduce-scatter.6.cloned.1.call-update) | async-done | bytes 2097168 | tf_op jit(solution)/shard_map/reduce_scatter | solution.py:96
  (36 shorter events, 2.9 us)
Async XLA Ops:
  7.2 34.7 %copy-start.2 = (bf16[128,1024]{1,0:T(8,128)(2,1)S(1)}, bf16[128,1024]{1,0:T(8,128)(2,1)}, u32[]{:S(2)}) copy-start(bf16[128,1024]{1,0:T(8,128)(2,1)} %param.7) | copy-start | bytes 786436
  7.2 88.7 %all-gather.3.cloned.1.call-start = ((), (), s32[]{:S(2)}) async-start(), calls=%async_computation.3 | async-start | bytes 5242880 | tf_op jit(solution)/shard_map/all_gather | solution.py:49
  7.9 134.1 %all-gather.5.cloned.1.call-start = ((), (), s32[]{:S(2)}) async-start(), calls=%async_computation.4 | async-start | bytes 2621440 | tf_op jit(solution)/shard_map/all_gather | solution.py:37
  8.7 231.3 %all-reduce.4.cloned.1.call-start = ((), (), s32[]{:S(2)}) async-start(), calls=%async_computation.5 | async-start | bytes 8388608 | tf_op jit(solution)/shard_map/psum | solution.py:78
  8.7 23.5 %collective-permute-start = (bf16[2,128,256]{2,1,0:T(8,128)(2,1)}, bf16[2,128,256]{2,1,0:T(8,128)(2,1)S(1)}, u32[]{:S(2)}, u32[]{:S(2)}) collective-permute-start(bf16[2,128,256]{2,1,0:T(8,128)(2,1)} %param.8), channel_id=1, source_target_pairs={{0,1},{1,2},{2,3},{3,0},{4,5},{5,6},{6,7},{7,4},{8,9},{9,10},{10,1... | collective-permute-start | bytes 393224 | tf_op jit(solution)/shard_map/ppermute | solution.py:16
  11.8 20.6 %collective-permute-start.1 = (bf16[2,128,256]{2,1,0:T(8,128)(2,1)}, bf16[2,128,256]{2,1,0:T(8,128)(2,1)S(1)}, u32[]{:S(2)}, u32[]{:S(2)}) collective-permute-start(bf16[2,128,256]{2,1,0:T(8,128)(2,1)} %param.8), channel_id=1, source_target_pairs={{0,3},{1,0},{2,1},{3,2},{4,7},{5,4},{6,5},{7,6},{8,11},{9,8},{10,9... | collective-permute-start | bytes 393224 | tf_op jit(solution)/shard_map/ppermute | solution.py:19
  32.3 9.6 %collective-permute-start.2 = (bf16[2,128,256]{2,1,0:T(8,128)(2,1)S(1)}, bf16[2,128,256]{2,1,0:T(8,128)(2,1)S(1)}, u32[]{:S(2)}, u32[]{:S(2)}) collective-permute-start(bf16[2,128,256]{2,1,0:T(8,128)(2,1)S(1)} %collective-permute-done), channel_id=1, source_target_pairs={{0,1},{1,2},{2,3},{3,0},{4,5},{5,6},{6,7},{7,4},{8,9},{9,10},{10,1... | collective-permute-start | bytes 393224 | tf_op jit(solution)/shard_map/ppermute | solution.py:16
  99.6 2.0 copy-start
  108.0 37.5 %copy-start.1 = (bf16[8,8,128,128]{2,3,1,0:T(8,128)(2,1)}, bf16[8,8,128,128]{2,3,1,0:T(8,128)(2,1)S(1)}, u32[]{:S(2)}) copy-start(bf16[8,8,128,128]{2,3,1,0:T(8,128)(2,1)S(1)} %copy.26) | copy-start | bytes 6291460
  142.0 2.8 copy-start.3
  144.7 5.6 %copy-start.4 = (bf16[128,8,128,1]{2,0,3,1:T(8,128)(2,1)}, bf16[128,8,128,1]{2,0,3,1:T(8,128)(2,1)S(1)}, u32[]{:S(2)}) copy-start(bf16[128,8,128,1]{2,0,3,1:T(8,128)(2,1)S(1)} %fusion.19) | copy-start | bytes 786436
  155.6 124.6 %reduce-scatter.4.cloned.1.call-start = ((), (), s32[]{:S(2)}) async-start(), calls=%async_computation.6 | async-start | bytes 1310720 | tf_op jit(solution)/shard_map/reduce_scatter | solution.py:94
  249.1 106.5 %reduce-scatter.8.cloned.1.call-start = ((), (), s32[]{:S(2)}) async-start(), calls=%async_computation.8 | async-start | bytes 5242880 | tf_op jit(solution)/shard_map/reduce_scatter | solution.py:95
  253.5 250.0 %reduce-scatter.6.cloned.1.call-start = ((), (), s32[]{:S(2)}) async-start(), calls=%async_computation.7 | async-start | bytes 10485760 | tf_op jit(solution)/shard_map/reduce_scatter | solution.py:96
  258.1 0.7 copy-start.5
Sparse Core Ops, SparseCore 0:
  9.6 86.2 all-gather.2
  97.5 44.4 all-gather.4
  155.7 84.1 all-reduce.3
  249.2 28.1 reduce-scatter.3
  280.1 75.4 reduce-scatter.7
  358.5 144.9 reduce-scatter.5
